TPU v7x, 512 devices: a whole 4x8x8 slice. The times are simulated.
512 devices in a mesh: ct: 128 (over y, z, core), bl: 4 (over x).
Axes of the slice: x: 4, y: 8, z: 8, core: 2. Of those that a mesh axis runs over, the one named last changes fastest.
Arguments:
- samples: bfloat16 [1024, 65536], P('ct', 'bl'), may hold values from -6 to 6
- history: bfloat16 [1024, 1536], P('ct'), may hold values from -6 to 6
- tile_cell: int32 [256, 36], P('ct'), may hold values from 0 to 7
- tile_weight: float32 [256, 36], P('ct'), may hold values from 0.25 to 4
Outputs:
- grid: float32 [8, 256, 2, 128, 128], P('bl', 'ct')
All inputs are finite; a program needn't handle non-finite values.
Results may differ from a plain program's by a relative error of at most 0.0048.
Values may be sent and summed in bfloat16 or wider, within the bound.
A program may use at most 64 MiB of HBM per device.

v0:
```python
import math
import jax
import jax.numpy as jnp
from jax import lax
from jax.sharding import PartitionSpec as P

CH = 256
BLOCK = 128
TAPS = 4
SPECTRA = 128
CELL_DEV = 2
FRAME = 512


def from_behind(value, axis, by):
    size = lax.axis_size(axis)
    pairs = [(i, i + by) for i in range(size) if 0 <= i + by < size]
    return lax.ppermute(value, axis, pairs)


def filter_table():
    span = TAPS * FRAME
    sample_pos = jnp.arange(span, dtype=jnp.float32) + 0.5
    window = jnp.sinc(sample_pos / FRAME - TAPS / 2.0) * (
        0.5 - 0.5 * jnp.cos(2.0 * math.pi * sample_pos / span)
    )
    phase_int = (
        jnp.arange(FRAME, dtype=jnp.int32)[:, None]
        * jnp.arange(CH, dtype=jnp.int32)[None, :]
        % FRAME
    )
    angle = phase_int.astype(jnp.float32) * (2.0 * math.pi / FRAME)
    basis = jnp.concatenate([jnp.cos(angle), -jnp.sin(angle)], axis=1)
    table = window.reshape(TAPS, FRAME)[:, :, None] * basis[None] * (2.0 / math.sqrt(FRAME))
    return table.astype(jnp.bfloat16)


def cell_selector(tile_cell, weights, tri_index, is_valid, cell_count):
    picked = jnp.take(tile_cell, tri_index, axis=1)
    picked_weight = jnp.take(weights, tri_index, axis=1) * is_valid
    cell_ids = lax.broadcasted_iota(jnp.int32, (cell_count, 1, 1), 0)
    return (picked[None] == cell_ids).astype(jnp.float32) * picked_weight[None]


def shards(samples, history, tile_cell, tile_weight):
    bl_size = lax.axis_size("bl")
    bl_index = lax.axis_index("bl")
    inputs_dev = samples.shape[0]
    spec_dev = samples.shape[1] // FRAME
    table = filter_table()
    frames = samples.reshape(inputs_dev, spec_dev, FRAME)
    last_frames = frames[:, spec_dev - (TAPS - 1) :, :]
    earlier = from_behind(last_frames, "bl", 1)
    earlier = jnp.where(bl_index == 0, history.reshape(inputs_dev, TAPS - 1, FRAME), earlier)
    extended = jnp.concatenate([earlier, frames], axis=1)
    accum = jnp.zeros((2 * CH, inputs_dev, spec_dev), jnp.float32)
    for tap_index in range(TAPS):
        accum = accum + jnp.einsum(
            "psn,nk->kps",
            extended[:, tap_index : tap_index + spec_dev],
            table[tap_index],
            preferred_element_type=jnp.float32,
        )
    spectra = accum.astype(jnp.bfloat16).reshape(2, CH, inputs_dev, spec_dev)
    turned = lax.all_to_all(spectra, "ct", split_axis=1, concat_axis=2, tiled=True)
    channels = turned.shape[1]
    inputs = turned.shape[2]
    blocks = inputs // BLOCK
    cell_count = CELL_DEV * bl_size
    weights = tile_weight * (1.0 / math.sqrt(SPECTRA))
    rows_each = blocks // bl_size
    shard_part = lax.all_gather(turned, "bl", axis=3, tiled=True)
    row_part = lax.dynamic_slice_in_dim(
        shard_part, bl_index * rows_each * BLOCK, rows_each * BLOCK, 2
    )
    products = jnp.einsum(
        "acps,bcqs->cabpq", row_part, shard_part, preferred_element_type=jnp.float32
    )
    visibility = jnp.stack(
        [products[:, 0, 0] + products[:, 1, 1], products[:, 1, 0] - products[:, 0, 1]], axis=1
    )
    visibility = visibility.reshape(channels, 2, rows_each, BLOCK, blocks, BLOCK)
    row_index = bl_index * rows_each + jnp.arange(rows_each, dtype=jnp.int32)
    col_index = jnp.arange(blocks, dtype=jnp.int32)
    is_valid = col_index[None, :] >= row_index[:, None]
    tri_index = (
        row_index[:, None] * blocks
        - row_index[:, None] * (row_index[:, None] - 1) // 2
        + col_index[None, :]
        - row_index[:, None]
    )
    tri_index = jnp.where(is_valid, tri_index, 0).reshape(-1)
    selector = cell_selector(
        tile_cell, weights, tri_index, is_valid.reshape(-1).astype(jnp.float32), cell_count
    )
    selector = selector.reshape(cell_count, channels, rows_each, blocks)
    cell_term = jnp.einsum(
        "ecmj,cxmpjq->ecxpq", selector, visibility, precision=lax.Precision.HIGHEST
    )
    return lax.psum_scatter(cell_term, "bl", scatter_dimension=0, tiled=True)


def solution(mesh):
    return jax.shard_map(
        shards,
        mesh=mesh,
        in_specs=(P("ct", "bl"), P("ct", None), P("ct", None), P("ct", None)),
        out_specs=P("bl", "ct", None, None, None),
        check_vma=False,
    )
```

profile of v0, /device:TPU:1, one launch (start us, length us, event | category | flops | bytes accessed | tf_op | source)
XLA Modules:
  0.0 138.1 jit_solution(12725136759354073979)
XLA Ops:
  6.5 1.0 copy.82
  7.6 3.9 %collective-permute-start = (bf16[8,3,512]{2,1,0:T(4,128)(2,1)S(1)}, bf16[8,3,512]{2,1,0:T(4,128)(2,1)S(1)}, u32[]{:S(2)}, u32[]{:S(2)}) collective-permute-start(bf16[8,3,512]{2,1,0:T(4,128)(2,1)S(1)} %slice.53), channel_id=1, source_target_pairs={{0,1},{1,2},{2,3},{4,5},{5,6},{6,7},{8,9},{9,10},{10,11},{12,13},{... | collective-permute-start | bytes 73736 | tf_op jit(solution)/shard_map/ppermute | solution.py:18
  11.6 2.1 %sine_negate_fusion = (f32[512,256]{1,0:T(8,128)S(1)}, f32[512,256]{1,0:T(8,128)S(1)}) fusion(), kind=kLoop, calls=%fused_computation.30 | loop fusion | flops 1966080 | bytes 1048576 | tf_op jit(solution)/shard_map/neg | solution.py:33
  13.9 0.4 multiply_convert_fusion
  14.3 0.5 copy-done
  15.2 0.4 copy-done.1
  16.7 1.1 copy.52
  17.8 0.8 reshape.324
  18.6 32.0 %all_to_all.18 = bf16[128,2,512]{2,1,0:T(2,128)(2,1)S(1)} all-to-all(bf16[128,2,512]{2,1,0:T(2,128)(2,1)S(1)} %reshape.324), channel_id=1, replica_groups=mesh['ct'=128,'bl'=4] {'ct'}, dimensions={0} | all-to-all | bytes 524288 | tf_op jit(solution)/shard_map/all_to_all | solution.py:65
  50.6 0.5 reshape.325
  51.3 1.2 copy.55
  53.3 0.6 gather_fusion.1
  54.0 0.6 gather_fusion
  54.8 19.1 %all-gather.2.cloned.1.call-done = bf16[2,2,1024,128]{2,1,0,3:T(2,128)(2,1)} async-done(((bf16[2,2,1024,32]{2,1,0,3:T(2,128)(2,1)}), bf16[2,2,1024,128]{2,1,0,3:T(2,128)(2,1)}) %all-gather.2.cloned.1.call-update) | async-done | bytes 1048592 | tf_op jit(solution)/shard_map/all_gather | solution.py:72
  73.9 1.1 constant_dynamic-slice_fusion
  75.3 2.5 %convolution_bitcast_fusion = f32[2,2,2,256,1024]{3,4,1,2,0:T(8,128)S(1)} fusion(bf16[2,2,1024,128,1]{2,1,0,3,4:T(2,128)(2,1)} %bitcast.68, bf16[2,2,256,128]{3,2,0,1:T(8,128)(2,1)S(1)} %copy.74), kind=kOutput, calls=%fused_computation.7 | convolution fusion | flops 536870912 | bytes 9699328 | tf_op jit(solution)/shard_map/acps,bcqs->cabpq/dot_general | solution.py:76
  77.8 2.5 %slice_add_fusion = (f32[2,1,1,256,1024]{3,4,1,2,0:T(8,128)}, f32[2,1,1,256,1024]{3,4,1,2,0:T(8,128)}) fusion(f32[2,2,2,256,1024]{3,4,1,2,0:T(8,128)S(1)} %convolution_bitcast_fusion), kind=kLoop, calls=%fused_computation.9 | loop fusion | flops 1048576 | bytes 12582912 | tf_op jit(solution)/shard_map/add | solution.py:80
  80.3 2.3 %add.221 = f32[2,1,2,128,8,128]{3,2,5,4,0,1:T(2,128)S(1)} reshape(f32[2,1,1,256,1024]{3,4,1,2,0:T(8,128)} %get-tuple-element.5) | data formatting | bytes 4194304 | tf_op jit(solution)/shard_map/add | solution.py:80
  82.6 2.0 %copy.58 = f32[2,1,2,128,8,128]{5,4,2,3,1,0:T(8,128)} copy(f32[2,1,2,128,8,128]{3,2,5,4,0,1:T(2,128)S(1)} %add.221) | data formatting | bytes 4194304 | tf_op jit(solution)/shard_map/add | solution.py:80
  84.6 2.3 %sub.83 = f32[2,1,2,128,8,128]{3,2,5,4,0,1:T(2,128)S(1)} reshape(f32[2,1,1,256,1024]{3,4,1,2,0:T(8,128)} %get-tuple-element.6) | data formatting | bytes 4194304 | tf_op jit(solution)/shard_map/sub | solution.py:80
  86.9 2.0 %copy.59 = f32[2,1,2,128,8,128]{5,4,2,3,1,0:T(8,128)} copy(f32[2,1,2,128,8,128]{3,2,5,4,0,1:T(2,128)S(1)} %sub.83) | data formatting | bytes 4194304 | tf_op jit(solution)/shard_map/sub | solution.py:80
  89.0 4.0 %fusion.4 = f32[8,2,2,128,128]{4,0,3,2,1:T(8,128)S(1)} fusion(f32[2,1,2,128,8,128]{5,4,2,3,1,0:T(8,128)} %copy.59, f32[2,1,2,128,8,128]{5,4,2,3,1,0:T(8,128)} %copy.58, f32[2,2,8]{2,1,0:T(2,128)S(1)} %select_multiply_fusion, s32[2,2,8]{2,1,0:T(2,128)S(1)} %broadcast_select_fusion.1), kind=kOutput, calls=%fused_computation.10 | convolution fusion | flops 101712384 | bytes 6291712 | tf_op jit(solution)/shard_map/ecmj,cxmpjq->ecxpq/dot_general | solution.py:97
  93.0 1.7 %copy.64 = f32[8,2,2,128,128]{4,3,2,1,0:T(8,128)} copy(f32[8,2,2,128,128]{4,0,3,2,1:T(8,128)S(1)} %fusion.4) | data formatting | bytes 4194304 | tf_op jit(solution)/shard_map/ecmj,cxmpjq->ecxpq/transpose | solution.py:97
  94.7 36.5 %reduce-scatter.2.cloned.1.call-done = f32[2,2,2,128,128]{4,3,2,1,0:T(8,128)} async-done(((f32[8,2,2,128,128]{4,3,2,1,0:T(8,128)}), f32[2,2,2,128,128]{4,3,2,1,0:T(8,128)}) %reduce-scatter.2.cloned.1.call-update) | async-done | bytes 524304 | tf_op jit(solution)/shard_map/reduce_scatter | solution.py:100
  (40 shorter events, 3.2 us)
Async XLA Ops:
  6.5 67.4 %all-gather.2.cloned.1.call-start = ((), (), s32[]{:S(2)}) async-start(), calls=%async_computation.2 | async-start | bytes 1310720 | tf_op jit(solution)/shard_map/all_gather | solution.py:72
  7.6 8.0 %collective-permute-start = (bf16[8,3,512]{2,1,0:T(4,128)(2,1)S(1)}, bf16[8,3,512]{2,1,0:T(4,128)(2,1)S(1)}, u32[]{:S(2)}, u32[]{:S(2)}) collective-permute-start(bf16[8,3,512]{2,1,0:T(4,128)(2,1)S(1)} %slice.53), channel_id=1, source_target_pairs={{0,1},{1,2},{2,3},{4,5},{5,6},{6,7},{8,9},{9,10},{10,11},{12,13},{... | collective-permute-start | bytes 73736 | tf_op jit(solution)/shard_map/ppermute | solution.py:18
  13.9 1.0 copy-start
  14.8 0.7 copy-start.1
  51.1 2.1 %copy-start.2 = (f32[2,36]{1,0:T(2,128)S(1)}, f32[2,36]{1,0:T(2,128)}, u32[]{:S(2)}) copy-start(f32[2,36]{1,0:T(2,128)} %param.7) | copy-start | bytes 868
  51.1 2.8 %copy-start.3 = (s32[2,36]{1,0:T(2,128)S(1)}, s32[2,36]{1,0:T(2,128)}, u32[]{:S(2)}) copy-start(s32[2,36]{1,0:T(2,128)} %param.6) | copy-start | bytes 868
  52.5 78.7 %reduce-scatter.2.cloned.1.call-start = ((), (), s32[]{:S(2)}) async-start(), calls=%async_computation.3 | async-start | bytes 2621440 | tf_op jit(solution)/shard_map/reduce_scatter | solution.py:100
Sparse Core Ops, SparseCore 0:
  52.6 21.2 all-gather.1
  94.9 36.3 reduce-scatter.1
where the time goes:
time: 138 us
  waiting for transfers between devices  55.6 us (40%)
  blocking collectives  32 us (23%)
  local copies, waits for them, and re-layouts  19.5 us (14%)
  between operations  13.6 us (10%)
  matrix products  7.79 us (6%)
  other arithmetic  5.36 us (4%)
  starting transfers between devices  4.17 us (3%)
    reduce_scatter x1, waiting for transfers between devices, shards(): return lax.psum_scatter(cell_term, 'bl', scatter_dimension=0, tiled=True)  36.5 us
    all_to_all x1, blocking collectives, shards(): lax.all_to_all(spectra, 'ct', split_axis=1, concat_axis=2, tiled=True)  32 us
    all_gather x1, waiting for transfers between devices, shards(): shard_part = lax.all_gather(turned, 'bl', axis=3, tiled=True)  19.1 us
    sub x2, local copies, waits for them, and re-layouts, shards(): products[:, 1, 0] - products[:, 0, 1]  4.33 us
    add x2, local copies, waits for them, and re-layouts, shards(): products[:, 0, 0] + products[:, 1, 1]  4.33 us
    dot_general x1, matrix products, shards(): jnp.einsum('ecmj,cxmpjq->ecxpq', selector, visibility, precision=lax.Prec...  4.02 us
    ppermute x1, starting transfers between devices, from_behind(): return lax.ppermute(value, axis, pairs)  3.95 us
    unnamed x13, local copies, waits for them, and re-layouts  3.65 us
  transfers between devices with their start and end apart: 3, of which 2 were waited for; matrix products, arithmetic and copies ran while one was open for 4% of the time, Pallas kernels for 0%

commit v1 on v0

--- a/solution.py
+++ b/solution.py
@@ -1,3 +1,4 @@
+import functools
 import math
 import jax
 import jax.numpy as jnp
@@ -10,6 +11,48 @@
 SPECTRA = 128
 CELL_DEV = 2
 FRAME = 512
+
+
+def cycles_play(incoming_x, where_dim):
+    incoming_x = jnp.moveaxis(incoming_x, 0, where_dim)
+    mat_out = incoming_x.shape
+    state_now = incoming_x.reshape(
+        *mat_out[:where_dim], mat_out[where_dim] * mat_out[where_dim + 1], *mat_out[where_dim + 2 :]
+    )
+    return state_now
+
+
+def search_copies(t0, named_axis, pos_dim):
+    n_shards = lax.axis_size(named_axis)
+    all_rows = []
+    it = 0
+    while it < n_shards:
+        all_rows.append((it, (it + 1) % n_shards))
+        it += 1
+    shelf = []
+    for ix, dd in all_rows:
+        shelf.append((dd, ix))
+    wide_out, y2 = ([], [])
+    k0 = 0
+    while k0 < n_shards - 1:
+        if k0 % 2 == 0:
+            wide_out.append(
+                lax.ppermute(wide_out[-1] if wide_out else t0, axis_name=named_axis, perm=all_rows)
+            )
+        else:
+            tmp = lax.ppermute(y2[-1] if y2 else t0, named_axis, shelf)
+            y2.append(tmp)
+        k0 = k0 + 1
+    last = jnp.stack([*wide_out[::-1], t0, *y2])
+    arr_out = lax.axis_index(named_axis)
+    taken_in = len(wide_out)
+    finding = arr_out - taken_in
+    last = last[(jnp.arange(n_shards) - finding) % n_shards]
+    b_now = cycles_play(last, pos_dim)
+    return b_now
+
+
+form_the_signs = functools.partial(search_copies, named_axis="bl", pos_dim=3)
 
 
 def from_behind(value, axis, by):
@@ -69,7 +112,7 @@
     cell_count = CELL_DEV * bl_size
     weights = tile_weight * (1.0 / math.sqrt(SPECTRA))
     rows_each = blocks // bl_size
-    shard_part = lax.all_gather(turned, "bl", axis=3, tiled=True)
+    shard_part = form_the_signs(turned)
     row_part = lax.dynamic_slice_in_dim(
         shard_part, bl_index * rows_each * BLOCK, rows_each * BLOCK, 2
     )

time: 138 us -> 127 us (0.920)
  blocking collectives: 32 us -> 0 us
  starting transfers between devices: 4.17 us -> 30.4 us
  waiting for transfers between devices: 55.6 us -> 51.4 us
    all_to_all x1 -> x0, blocking collectives: 32 us -> none  [shards(): lax.all_to_all(spectra, 'ct', split_axis=1, concat_axis=2, tiled=True)]
    all_gather x1 -> x0, waiting for transfers between devices: 19.1 us -> none  [shards(): shard_part = lax.all_gather(turned, 'bl', axis=3, tiled=True)]
    all_to_all x0 -> x1, starting transfers between devices: none -> 17.9 us  [shards(): lax.all_to_all(spectra, 'ct', split_axis=1, concat_axis=2, tiled=True)]
    all_to_all x0 -> x1, waiting for transfers between devices: none -> 14.1 us  [shards(): lax.all_to_all(spectra, 'ct', split_axis=1, concat_axis=2, tiled=True)]
    ppermute x0 -> x3, starting transfers between devices: none -> 8.57 us  [the longest x2 5.2 us: search_copies(): lax.ppermute(wide_out[-1] if wide_out else t0, axis_name=named_axis, perm...]
    ppermute x0 -> x3, waiting for transfers between devices: none -> 6.94 us  [the longest x2 6.93 us: search_copies(): lax.ppermute(wide_out[-1] if wide_out else t0, axis_name=named_axis, perm...]
    reduce_scatter x1, waiting for transfers between devices: 36.5 us -> 30.4 us  [shards(): return lax.psum_scatter(cell_term, 'bl', scatter_dimension=0, tiled=True)]
  transfers between devices with their start and end apart: 3 -> 6, of which waited for: 2 -> 4; matrix products, arithmetic and copies ran while one was open for 4% -> 4% of each run, Pallas kernels for 0% -> 0%
where the time goes in v1:
time: 127 us; the launch traced here: 126 us
  waiting for transfers between devices  51.4 us (40%)
  starting transfers between devices  30.4 us (24%)
  local copies, waits for them, and re-layouts  18.8 us (15%)
  between operations  13.7 us (11%)
  matrix products  6.56 us (5%)
  other arithmetic  5.52 us (4%)
    reduce_scatter x1, waiting for transfers between devices, shards(): return lax.psum_scatter(cell_term, 'bl', scatter_dimension=0, tiled=True)  30.4 us
    all_to_all x1, starting transfers between devices, shards(): lax.all_to_all(spectra, 'ct', split_axis=1, concat_axis=2, tiled=True)  17.9 us
    all_to_all x1, waiting for transfers between devices, shards(): lax.all_to_all(spectra, 'ct', split_axis=1, concat_axis=2, tiled=True)  14.1 us
    ppermute x2, waiting for transfers between devices, search_copies(): lax.ppermute(wide_out[-1] if wide_out else t0, axis_name=named_axis, perm...  6.93 us
    ppermute x2, starting transfers between devices, search_copies(): lax.ppermute(wide_out[-1] if wide_out else t0, axis_name=named_axis, perm...  5.2 us
    sub x2, local copies, waits for them, and re-layouts, shards(): products[:, 1, 0] - products[:, 0, 1]  4.33 us
    add x2, local copies, waits for them, and re-layouts, shards(): products[:, 0, 0] + products[:, 1, 1]  4.32 us
    dot_general x1, matrix products, shards(): jnp.einsum('ecmj,cxmpjq->ecxpq', selector, visibility, precision=lax.Prec...  4.02 us
  transfers between devices with their start and end apart: 6, of which 4 were waited for; matrix products, arithmetic and copies ran while one was open for 4% of the time, Pallas kernels for 0%

profile of v1, /device:TPU:1, one launch (start us, length us, event | category | flops | bytes accessed | tf_op | source)
XLA Modules:
  0.0 126.5 jit_solution(2275532657703800407)
XLA Ops:
  6.5 1.0 copy.84
  7.6 3.9 %collective-permute-start = (bf16[8,3,512]{2,1,0:T(4,128)(2,1)S(1)}, bf16[8,3,512]{2,1,0:T(4,128)(2,1)S(1)}, u32[]{:S(2)}, u32[]{:S(2)}) collective-permute-start(bf16[8,3,512]{2,1,0:T(4,128)(2,1)S(1)} %slice.55), channel_id=1, source_target_pairs={{0,1},{1,2},{2,3},{4,5},{5,6},{6,7},{8,9},{9,10},{10,11},{12,13},{... | collective-permute-start | bytes 73736 | tf_op jit(solution)/shard_map/ppermute | solution.py:61
  11.6 2.1 %sine_negate_fusion = (f32[512,256]{1,0:T(8,128)S(1)}, f32[512,256]{1,0:T(8,128)S(1)}) fusion(), kind=kLoop, calls=%fused_computation.33 | loop fusion | flops 1966080 | bytes 1048576 | tf_op jit(solution)/shard_map/neg | solution.py:76
  16.7 1.1 copy.48
  17.8 1.5 %reshape.386 = bf16[128,2,512]{2,1,0:T(2,128)(2,1)} reshape(bf16[256,2,8,32]{3,2,1,0:T(8,128)(2,1)S(1)} %bitcast.82) | data formatting | bytes 524288
  19.3 17.9 %all-to-all-start = ((bf16[128,2,512]{2,1,0:T(2,128)(2,1)}), bf16[128,2,512]{2,1,0:T(2,128)(2,1)S(1)}, u32[]{:S(2)}, u32[]{:S(2)}) async-start(bf16[128,2,512]{2,1,0:T(2,128)(2,1)} %reshape.386), calls=%async_computation | async-start | bytes 524288 | tf_op jit(solution)/shard_map/all_to_all | solution.py:108
  37.4 14.1 %all-to-all-done = bf16[128,2,512]{2,1,0:T(2,128)(2,1)S(1)} async-done(((bf16[128,2,512]{2,1,0:T(2,128)(2,1)}), bf16[128,2,512]{2,1,0:T(2,128)(2,1)S(1)}, u32[]{:S(2)}, u32[]{:S(2)}) %all-to-all-start) | async-done | bytes 262176 | tf_op jit(solution)/shard_map/all_to_all | solution.py:108
  52.5 3.1 %collective-permute-start.1 = (bf16[2,2,1024,32]{2,3,1,0:T(8,128)(2,1)S(1)}, bf16[2,2,1024,32]{2,3,1,0:T(8,128)(2,1)S(1)}, u32[]{:S(2)}, u32[]{:S(2)}) collective-permute-start(bf16[2,2,1024,32]{2,3,1,0:T(8,128)(2,1)S(1)} %copy.51), channel_id=1, source_target_pairs={{0,1},{1,2},{2,3},{3,0},{4,5},{5,6},{6,7},{7,4},{8,9},{9,10},{10,1... | collective-permute-start | bytes 786440 | tf_op jit(solution)/shard_map/ppermute | solution.py:40
  55.7 0.6 gather_fusion.1
  56.4 3.4 %collective-permute-start.3 = (bf16[2,2,1024,32]{2,3,1,0:T(8,128)(2,1)S(1)}, bf16[2,2,1024,32]{2,3,1,0:T(8,128)(2,1)S(1)}, u32[]{:S(2)}, u32[]{:S(2)}) collective-permute-start(bf16[2,2,1024,32]{2,3,1,0:T(8,128)(2,1)S(1)} %copy.51), channel_id=1, source_target_pairs={{1,0},{2,1},{3,2},{0,3},{5,4},{6,5},{7,6},{4,7},{9,8},{10,9},{11,1... | collective-permute-start | bytes 786440 | tf_op jit(solution)/shard_map/ppermute | solution.py:43
  59.8 1.8 %collective-permute-done.1 = bf16[2,2,1024,32]{2,3,1,0:T(8,128)(2,1)S(1)} collective-permute-done((bf16[2,2,1024,32]{2,3,1,0:T(8,128)(2,1)S(1)}, bf16[2,2,1024,32]{2,3,1,0:T(8,128)(2,1)S(1)}, u32[]{:S(2)}, u32[]{:S(2)}) %collective-permute-start.1) | collective-permute-done | bytes 262176 | tf_op jit(solution)/shard_map/ppermute | solution.py:40
  61.6 2.1 %collective-permute-start.2 = (bf16[2,2,1024,32]{2,3,1,0:T(8,128)(2,1)S(1)}, bf16[2,2,1024,32]{2,3,1,0:T(8,128)(2,1)S(1)}, u32[]{:S(2)}, u32[]{:S(2)}) collective-permute-start(bf16[2,2,1024,32]{2,3,1,0:T(8,128)(2,1)S(1)} %collective-permute-done.1), channel_id=1, source_target_pairs={{0,1},{1,2},{2,3},{3,0},{4,5},{5,6},{6,7},{7,4},{8,9},{9,10},{10,1... | collective-permute-start | bytes 786440 | tf_op jit(solution)/shard_map/ppermute | solution.py:40
  63.8 0.6 gather_fusion.2
  64.8 5.1 %collective-permute-done.2 = bf16[2,2,1024,32]{2,3,1,0:T(8,128)(2,1)S(1)} collective-permute-done((bf16[2,2,1024,32]{2,3,1,0:T(8,128)(2,1)S(1)}, bf16[2,2,1024,32]{2,3,1,0:T(8,128)(2,1)S(1)}, u32[]{:S(2)}, u32[]{:S(2)}) %collective-permute-start.2) | collective-permute-done | bytes 262176 | tf_op jit(solution)/shard_map/ppermute | solution.py:40
  70.0 0.6 gather_fusion
  71.0 1.3 %convolution_bitcast_fusion = f32[2,2,2,256,1024]{3,4,1,2,0:T(8,128)S(1)} fusion(bf16[2,2,1024,128,1]{2,3,1,0,4:T(8,128)(2,1)S(1)} %bitcast.81, bf16[2,2,256,128]{3,2,0,1:T(8,128)(2,1)S(1)} %copy.75), kind=kOutput, calls=%fused_computation.8 | convolution fusion | flops 536870912 | bytes 9699328 | tf_op jit(solution)/shard_map/acps,bcqs->cabpq/dot_general | solution.py:119
  72.3 2.5 %slice_add_fusion = (f32[2,1,1,256,1024]{3,4,1,2,0:T(8,128)}, f32[2,1,1,256,1024]{3,4,1,2,0:T(8,128)}) fusion(f32[2,2,2,256,1024]{3,4,1,2,0:T(8,128)S(1)} %convolution_bitcast_fusion), kind=kLoop, calls=%fused_computation.10 | loop fusion | flops 1048576 | bytes 12582912 | tf_op jit(solution)/shard_map/add | solution.py:123
  74.8 2.3 %add.247 = f32[2,1,2,128,8,128]{3,2,5,4,0,1:T(2,128)S(1)} reshape(f32[2,1,1,256,1024]{3,4,1,2,0:T(8,128)} %get-tuple-element.5) | data formatting | bytes 4194304 | tf_op jit(solution)/shard_map/add | solution.py:123
  77.1 2.0 %copy.58 = f32[2,1,2,128,8,128]{5,4,2,3,1,0:T(8,128)} copy(f32[2,1,2,128,8,128]{3,2,5,4,0,1:T(2,128)S(1)} %add.247) | data formatting | bytes 4194304 | tf_op jit(solution)/shard_map/add | solution.py:123
  79.1 2.3 %sub.102 = f32[2,1,2,128,8,128]{3,2,5,4,0,1:T(2,128)S(1)} reshape(f32[2,1,1,256,1024]{3,4,1,2,0:T(8,128)} %get-tuple-element.6) | data formatting | bytes 4194304 | tf_op jit(solution)/shard_map/sub | solution.py:123
  81.4 2.0 %copy.59 = f32[2,1,2,128,8,128]{5,4,2,3,1,0:T(8,128)} copy(f32[2,1,2,128,8,128]{3,2,5,4,0,1:T(2,128)S(1)} %sub.102) | data formatting | bytes 4194304 | tf_op jit(solution)/shard_map/sub | solution.py:123
  83.4 4.0 %fusion.4 = f32[8,2,2,128,128]{4,0,3,2,1:T(8,128)S(1)} fusion(f32[2,1,2,128,8,128]{5,4,2,3,1,0:T(8,128)} %copy.59, f32[2,1,2,128,8,128]{5,4,2,3,1,0:T(8,128)} %copy.58, f32[2,2,8]{2,1,0:T(2,128)S(1)} %select_multiply_fusion, s32[2,2,8]{2,1,0:T(2,128)S(1)} %broadcast_select_fusion.1), kind=kOutput, calls=%fused_computation.11 | convolution fusion | flops 101712384 | bytes 6291712 | tf_op jit(solution)/shard_map/ecmj,cxmpjq->ecxpq/dot_general | solution.py:140
  87.5 1.7 %copy.64 = f32[8,2,2,128,128]{4,3,2,1,0:T(8,128)} copy(f32[8,2,2,128,128]{4,0,3,2,1:T(8,128)S(1)} %fusion.4) | data formatting | bytes 4194304 | tf_op jit(solution)/shard_map/ecmj,cxmpjq->ecxpq/transpose | solution.py:140
  89.2 30.4 %reduce-scatter.2.cloned.1.call-done = f32[2,2,2,128,128]{4,3,2,1,0:T(8,128)} async-done(((f32[8,2,2,128,128]{4,3,2,1,0:T(8,128)}), f32[2,2,2,128,128]{4,3,2,1,0:T(8,128)}) %reduce-scatter.2.cloned.1.call-update) | async-done | bytes 524304 | tf_op jit(solution)/shard_map/reduce_scatter | solution.py:143
  (50 shorter events, 5.3 us)
Async XLA Ops:
  7.6 8.0 %collective-permute-start = (bf16[8,3,512]{2,1,0:T(4,128)(2,1)S(1)}, bf16[8,3,512]{2,1,0:T(4,128)(2,1)S(1)}, u32[]{:S(2)}, u32[]{:S(2)}) collective-permute-start(bf16[8,3,512]{2,1,0:T(4,128)(2,1)S(1)} %slice.55), channel_id=1, source_target_pairs={{0,1},{1,2},{2,3},{4,5},{5,6},{6,7},{8,9},{9,10},{10,11},{12,13},{... | collective-permute-start | bytes 73736 | tf_op jit(solution)/shard_map/ppermute | solution.py:61
  13.9 1.0 copy-start
  14.8 0.7 copy-start.1
  16.6 20.7 %copy-start.2 = (f32[2,36]{1,0:T(2,128)S(1)}, f32[2,36]{1,0:T(2,128)}, u32[]{:S(2)}) copy-start(f32[2,36]{1,0:T(2,128)} %param.7) | copy-start | bytes 868
  19.3 32.1 %all-to-all-start = ((bf16[128,2,512]{2,1,0:T(2,128)(2,1)}), bf16[128,2,512]{2,1,0:T(2,128)(2,1)S(1)}, u32[]{:S(2)}, u32[]{:S(2)}) async-start(bf16[128,2,512]{2,1,0:T(2,128)(2,1)} %reshape.386), calls=%async_computation | async-start | bytes 524288 | tf_op jit(solution)/shard_map/all_to_all | solution.py:108
  37.2 82.4 %reduce-scatter.2.cloned.1.call-start = ((), (), s32[]{:S(2)}) async-start(), calls=%async_computation.2 | async-start | bytes 2621440 | tf_op jit(solution)/shard_map/reduce_scatter | solution.py:143
  37.4 18.2 %copy-start.3 = (s32[2,36]{1,0:T(2,128)S(1)}, s32[2,36]{1,0:T(2,128)}, u32[]{:S(2)}) copy-start(s32[2,36]{1,0:T(2,128)} %param.6) | copy-start | bytes 868
  52.5 9.1 %collective-permute-start.1 = (bf16[2,2,1024,32]{2,3,1,0:T(8,128)(2,1)S(1)}, bf16[2,2,1024,32]{2,3,1,0:T(8,128)(2,1)S(1)}, u32[]{:S(2)}, u32[]{:S(2)}) collective-permute-start(bf16[2,2,1024,32]{2,3,1,0:T(8,128)(2,1)S(1)} %copy.51), channel_id=1, source_target_pairs={{0,1},{1,2},{2,3},{3,0},{4,5},{5,6},{6,7},{7,4},{8,9},{9,10},{10,1... | collective-permute-start | bytes 786440 | tf_op jit(solution)/shard_map/ppermute | solution.py:40
  56.4 8.4 %collective-permute-start.3 = (bf16[2,2,1024,32]{2,3,1,0:T(8,128)(2,1)S(1)}, bf16[2,2,1024,32]{2,3,1,0:T(8,128)(2,1)S(1)}, u32[]{:S(2)}, u32[]{:S(2)}) collective-permute-start(bf16[2,2,1024,32]{2,3,1,0:T(8,128)(2,1)S(1)} %copy.51), channel_id=1, source_target_pairs={{1,0},{2,1},{3,2},{0,3},{5,4},{6,5},{7,6},{4,7},{9,8},{10,9},{11,1... | collective-permute-start | bytes 786440 | tf_op jit(solution)/shard_map/ppermute | solution.py:43
  61.6 8.3 %collective-permute-start.2 = (bf16[2,2,1024,32]{2,3,1,0:T(8,128)(2,1)S(1)}, bf16[2,2,1024,32]{2,3,1,0:T(8,128)(2,1)S(1)}, u32[]{:S(2)}, u32[]{:S(2)}) collective-permute-start(bf16[2,2,1024,32]{2,3,1,0:T(8,128)(2,1)S(1)} %collective-permute-done.1), channel_id=1, source_target_pairs={{0,1},{1,2},{2,3},{3,0},{4,5},{5,6},{6,7},{7,4},{8,9},{9,10},{10,1... | collective-permute-start | bytes 786440 | tf_op jit(solution)/shard_map/ppermute | solution.py:40
Sparse Core Ops, SparseCore 0:
  89.3 30.2 reduce-scatter.1
